TPU v7x, 512 devices: a whole 4x4x16 slice. The times are simulated.
512 devices in a mesh: slot: 16 (over y_hi, x, core), blk: 32 (over z, y_lo).
Axes of the slice: x: 4, y: 4 (y_hi: 2, y_lo: 2; y = y_hi * 2 + y_lo), z: 16, core: 2. Of those that a mesh axis runs over, the one named last changes fastest.
Arguments:
- owner: int32 [16], replicated, may hold values from 0 to 15, as said below
- factor: float32 [16, 3584, 3584], P('slot', 'blk'), may hold values from -0.09375 to 0.09375
- inverse_old: bfloat16 [16, 3584, 3584], P('slot', 'blk'), may hold values from -1 to 1
- acts_t: bfloat16 [16, 3584, 640], P('slot', 'blk'), may hold values from -6 to 6
- damping: float32 [16], P('slot'), may hold values from 0.5 to 2
Outputs:
- refreshed: bfloat16 [16, 3584, 640], P('slot', 'blk')
Inputs may be any that keep to these rules, and one draw needn't show every extreme that they name: owner names every index of slot exactly once, and for at least one layer l, owner[l] = (l + 8) mod 16.
All inputs are finite; a program needn't handle non-finite values.
Results may differ from a plain program's by a relative error of at most 0.0049.
Values may be sent and summed in bfloat16 or wider, within the bound.
A program may use at most 64 MiB of HBM per device.

v0:
```python
import jax
import jax.numpy as jnp
from jax import lax
from jax.sharding import PartitionSpec as P

COLS = 640


beta_keep = 0.75


def shards(owner, factor, inverse_old, acts_t, damping):
    factor_panel = factor[0]
    inverse_panel = inverse_old[0]
    acts_panel = acts_t[0]
    damp_value = damping[0]
    panel_rows = factor_panel.shape[0]
    width_all = factor_panel.shape[1]
    tok_count = acts_panel.shape[1]
    window = inverse_panel[:, :COLS]
    outer_cols = jnp.dot(
        acts_panel,
        lax.all_gather(acts_panel, "blk", axis=0, tiled=True).T,
        preferred_element_type=jnp.float32,
    )
    first_own = lax.axis_index("blk") * panel_rows
    row_ids = lax.broadcasted_iota(jnp.int32, (panel_rows, width_all), 0) + first_own
    col_ids = lax.broadcasted_iota(jnp.int32, (panel_rows, width_all), 1)
    identity_panel = jnp.where(row_ids == col_ids, 1.0, 0.0).astype(jnp.float32)
    damped_panel = (
        beta_keep * factor_panel
        + (1.0 - beta_keep) / tok_count * outer_cols
        + damp_value * identity_panel
    )
    column_block = damped_panel
    applied_full = jnp.dot(
        column_block,
        lax.all_gather(window, "blk", axis=0, tiled=True).astype(jnp.float32),
        precision=lax.Precision.HIGHEST,
    )
    applied = applied_full.astype(jnp.bfloat16)
    column_block = inverse_panel
    product = jnp.dot(
        column_block,
        lax.all_gather(applied, "blk", axis=0, tiled=True),
        preferred_element_type=jnp.float32,
    )
    refreshed_panel = (2.0 * window.astype(jnp.float32) - product).astype(jnp.bfloat16)
    slot_here = lax.axis_index("slot")
    slot_ids = jnp.arange(owner.shape[0], dtype=jnp.int32)
    target = jnp.sum(jnp.where(slot_ids == slot_here, owner, 0))
    shard_piece = lax.all_gather(refreshed_panel[None], "slot", axis=0, tiled=True)
    piece_ids = jnp.arange(shard_piece.shape[0], dtype=jnp.int32)
    chosen = piece_ids == target
    delivered = jnp.sum(
        jnp.where(chosen[:, None, None], shard_piece.astype(jnp.float32), 0.0), axis=0
    )
    return delivered.astype(jnp.bfloat16)[None]


def solution(mesh):
    placed = (
        P(),
        P("slot", "blk", None),
        P("slot", "blk", None),
        P("slot", "blk", None),
        P("slot"),
    )
    return jax.shard_map(
        shards, mesh=mesh, in_specs=placed, out_specs=P("slot", "blk", None), check_vma=False
    )
```

profile of v0, /device:TPU:1, one launch (start us, length us, event | category | flops | bytes accessed | tf_op | source)
XLA Modules:
  0.0 519.7 jit_solution(363442987958433220)
XLA Ops:
  6.5 0.0 all-gather.11.cloned.1.call-start
  6.5 0.7 all-gather.11.cloned.1.call-update
  7.3 0.0 all-gather.7.cloned.1.call-start
  7.3 1.6 slice.4
  8.9 0.0 all-gather.7.cloned.1.call-update
  8.9 0.0 all-gather.9.cloned.1.call-start
  9.6 130.8 %all-gather.11.cloned.1.call-done = bf16[1,3584,640]{2,1,0:T(8,128)(2,1)} async-done(((bf16[1,112,640]{2,1,0:T(8,128)(2,1)}), bf16[1,3584,640]{2,1,0:T(8,128)(2,1)}) %all-gather.11.cloned.1.call-update) | async-done | bytes 4587536 | tf_op jit(solution)/shard_map/all_gather | solution.py:23
  140.5 4.4 fusion.1
  144.9 0.0 copy-start
  144.9 137.3 %all-gather.7.cloned.1.call-done = bf16[3584,640]{1,0:T(8,128)(2,1)} async-done(((bf16[112,640]{1,0:T(8,128)(2,1)}), bf16[3584,640]{1,0:T(8,128)(2,1)}) %all-gather.7.cloned.1.call-update) | async-done | bytes 4587536 | tf_op jit(solution)/shard_map/all_gather | solution.py:38
  282.3 5.2 %convolution_convert_fusion = bf16[112,640]{1,0:T(8,128)(2,1)} fusion(f32[112,3584]{1,0:T(8,128)S(1)} %fusion.1, bf16[3584,640]{1,0:T(8,128)(2,1)} %all-gather.7.cloned.1.call-done), kind=kOutput, calls=%fused_computation.10 | convolution fusion | flops 3082885120 | bytes 6336512 | tf_op jit(solution)/shard_map/dot_general | solution.py:36
  287.5 0.0 all-gather.9.cloned.1.call-update
  287.5 0.0 copy-start.1
  287.5 0.0 all-gather.13.cloned.1.call-start
  287.6 139.8 %all-gather.9.cloned.1.call-done = bf16[3584,640]{1,0:T(8,128)(2,1)} async-done(((bf16[112,640]{1,0:T(8,128)(2,1)}), bf16[3584,640]{1,0:T(8,128)(2,1)}) %all-gather.9.cloned.1.call-update) | async-done | bytes 4587536 | tf_op jit(solution)/shard_map/all_gather | solution.py:45
  427.3 0.0 copy-done
  427.4 3.8 fusion.5
  431.2 0.0 all-gather.13.cloned.1.call-update
  431.2 0.0 copy-done.1
  431.2 0.6 fusion.7
  431.9 0.6 iota_compare_fusion.1
  432.4 77.9 %all-gather.13.cloned.1.call-done = bf16[1792,640]{1,0:T(8,128)(2,1)} async-done(((bf16[112,640]{1,0:T(8,128)(2,1)}), bf16[1792,640]{1,0:T(8,128)(2,1)}) %all-gather.13.cloned.1.call-update) | async-done | bytes 2293776 | tf_op jit(solution)/shard_map/all_gather | solution.py:52
  510.4 2.9 fusion.2
  (1 shorter events, 0.0 us)
Async XLA Ops:
  6.5 133.9 %all-gather.11.cloned.1.call-start = ((), (), s32[]{:S(2)}) async-start(), calls=%async_computation.2 | async-start | bytes 4730880 | tf_op jit(solution)/shard_map/all_gather | solution.py:23
  7.3 275.0 %all-gather.7.cloned.1.call-start = ((), (), s32[]{:S(2)}) async-start(), calls=%async_computation | async-start | bytes 4730880 | tf_op jit(solution)/shard_map/all_gather | solution.py:38
  8.9 418.4 %all-gather.9.cloned.1.call-start = ((), (), s32[]{:S(2)}) async-start(), calls=%async_computation.1 | async-start | bytes 4730880 | tf_op jit(solution)/shard_map/all_gather | solution.py:45
  144.9 282.4 %copy-start = (bf16[1,112,3584]{2,1,0:T(8,128)(2,1)S(1)}, bf16[1,112,3584]{2,1,0:T(8,128)(2,1)}, u32[]{:S(2)}) copy-start(bf16[1,112,3584]{2,1,0:T(8,128)(2,1)} %param.7) | copy-start | bytes 2408452
  287.5 143.7 %copy-start.1 = (s32[16]{0:T(128)S(1)}, s32[16]{0:T(128)}, u32[]{:S(2)}) copy-start(s32[16]{0:T(128)} %param.5) | copy-start | bytes 196
  287.5 222.8 %all-gather.13.cloned.1.call-start = ((), (), s32[]{:S(2)}) async-start(), calls=%async_computation.3 | async-start | bytes 2437120 | tf_op jit(solution)/shard_map/all_gather | solution.py:52
Sparse Core Ops, SparseCore 0:
  9.4 130.9 all-gather.10
  142.5 139.6 all-gather.6
  287.6 139.6 all-gather.8
  431.3 78.9 all-gather.12
where the time goes:
time: 520 us
  waiting for transfers between devices  487 us (94%)
  between operations  13.8 us (3%)
  matrix products  13.5 us (3%)
    all_gather x1, waiting for transfers between devices, shards(): lax.all_gather(applied, 'blk', axis=0, tiled=True)  140 us
    all_gather x1, waiting for transfers between devices, shards(): lax.all_gather(window, 'blk', axis=0, tiled=True).astype(jnp.float32)  137 us
    all_gather x1, waiting for transfers between devices, shards(): lax.all_gather(acts_panel, 'blk', axis=0, tiled=True)  131 us
    all_gather x1, waiting for transfers between devices, shards(): lax.all_gather(refreshed_panel[None], 'slot', axis=0, tiled=True)  77.9 us
  transfers between devices with their start and end apart: 4, of which 4 were waited for; matrix products, arithmetic and copies ran while one was open for 1% of the time, Pallas kernels for 0%

commit v1 on v0

v1 whole, which is shorter than its diff:
```python
import jax
import jax.numpy as jnp
from jax import lax
from jax.experimental import pallas as pl
from jax.experimental.pallas import tpu as pltpu
from jax.sharding import PartitionSpec as P

COLS = 640
TOK = 640
BETA = 0.75
NZ = 16
NS = 16
ROWS = 112
KP = 128
PIECES = 7
MESH = pl.DeviceIdType.MESH
HOPS = NZ // 2
PARTS = ((0, 256), (256, 384))


def wait_for(ref, sem):
    pltpu.make_async_copy(ref, ref, sem).wait()


def kernel(
    owner, damping, factor, inverse, acts, out,
    f_in, p_in, f_out, p_out, f_work, p_work, a_own,
    w_ring, a_ring, x_ring, total, sibling_part, damp_out, damp_in,
    gathered, picked, load_sem,
    swap_send, swap_recv, ring_send, ring_recv, pair_send, pair_recv,
    give_send, give_recv, pick_send, pick_recv,
):
    slot = lax.axis_index("slot")
    blk = lax.axis_index("blk")
    chip = slot // 2
    core = slot % 2
    z = blk // 2
    side = blk % 2
    same = core == side

    def at(core_at, side_at, z_at):
        return (chip * 2 + core_at, z_at * 2 + side_at)

    sibling = at(1 - core, side, z)
    up = at(core, side, (z + 1) % NZ)
    down = at(core, side, (z + NZ - 1) % NZ)

    f_load = pltpu.make_async_copy(factor.at[0], f_in, load_sem.at[0])
    p_load = pltpu.make_async_copy(inverse.at[0], p_in, load_sem.at[1])
    f_load.start()
    p_load.start()

    barrier = pltpu.get_barrier_semaphore()
    pl.semaphore_signal(barrier, inc=1, device_id=up, device_id_type=MESH)
    pl.semaphore_signal(barrier, inc=1, device_id=down, device_id_type=MESH)

    def greet(i, carry):
        @pl.when(jnp.logical_or(i // 2 != slot, i % 2 != side))
        def _():
            pl.semaphore_signal(
                barrier, inc=1, device_id=(i // 2, z * 2 + i % 2), device_id_type=MESH
            )
        return carry

    lax.fori_loop(0, 2 * NS, greet, 0)

    pad = jnp.zeros((KP - ROWS, COLS), jnp.bfloat16)

    def clear(i, carry):
        w_ring[i, ROWS:KP, :] = pad
        a_ring[i, ROWS:KP, :] = pad
        x_ring[i, ROWS:KP, :] = pad
        return carry

    lax.fori_loop(0, NZ, clear, 0)
    pl.semaphore_wait(barrier, 2 * NS + 1)

    def deliver(src, dst, send, recv, target, own):
        @pl.when(own)
        def _():
            pltpu.make_async_copy(src, dst, recv).start()

        @pl.when(jnp.logical_not(own))
        def _():
            pltpu.make_async_remote_copy(
                src_ref=src, dst_ref=dst, send_sem=send, recv_sem=recv,
                device_id=target, device_id_type=MESH,
            ).start()

    def sent(src, send, own):
        @pl.when(jnp.logical_not(own))
        def _():
            wait_for(src, send)

    w_home = inverse.at[0, :, pl.ds(0, COLS)]
    a_home = acts.at[0]
    deliver(
        w_home, w_ring.at[z, pl.ds(0, ROWS)], swap_send.at[0], swap_recv.at[0],
        at(side, core, z), same,
    )
    own_rows = pl.ds(pl.multiple_of(side * ROWS, 16), ROWS)
    for q in range(2):
        deliver(
            a_home, a_own.at[own_rows], swap_send.at[1 + q], swap_recv.at[1 + side],
            at(q, core, z), jnp.logical_and(same, core == q),
        )

    damp_out[...] = jnp.full((8, 128), damping[0], jnp.float32)

    @pl.when(same)
    def _():
        damp_in[...] = damp_out[...]
        pltpu.make_async_remote_copy(
            src_ref=damp_out, dst_ref=damp_in, send_sem=swap_send.at[7],
            recv_sem=swap_recv.at[7], device_id=sibling, device_id_type=MESH,
        ).start()

    def relayout(src, dst):
        for j in range(2 * NZ):
            start = ROWS * j
            base = start // 128 * 128
            off = start - base
            if off == 0:
                piece = src[:, base : base + 128].astype(jnp.bfloat16)
            elif off + ROWS <= 128:
                piece = pltpu.roll(
                    src[:, base : base + 128].astype(jnp.float32), 128 - off, 1
                ).astype(jnp.bfloat16)
            else:
                piece = pltpu.roll(
                    src[:, base : base + 256].astype(jnp.float32), 256 - off, 1
                )[:, :128].astype(jnp.bfloat16)
            dst[j % 2, j // 2] = piece

    def send_panel(src, dst, first):
        for q in range(2):
            deliver(
                src.at[q], dst.at[:, own_rows], swap_send.at[first + q],
                swap_recv.at[first + side],
                at(q, core, z), jnp.logical_and(same, core == q),
            )

    f_load.wait()
    relayout(f_in, f_out)
    send_panel(f_out, f_work, 3)

    def ring_copy(stream, ref, place, way, hop):
        return pltpu.make_async_remote_copy(
            src_ref=ref, dst_ref=ref, send_sem=ring_send.at[stream, way, hop],
            recv_sem=ring_recv.at[stream, place],
            device_id=up if way == 0 else down, device_id_type=MESH,
        )

    def ring_ref(stream, place):
        if stream == 0:
            return w_ring.at[place, pl.ds(0, ROWS)]
        if stream == 1:
            return a_ring.at[place, pl.ds(0, ROWS)]
        first, width = PARTS[stream - 2]
        return x_ring.at[place, pl.ds(0, ROWS), pl.ds(first, width)]

    def far(stream):
        return (HOPS, HOPS - 1) if stream % 2 == 0 else (HOPS - 1, HOPS)

    def step(stream, hop):
        for way in range(2):
            if hop <= far(stream)[way]:
                place = (z - hop + NZ) % NZ if way == 0 else (z + hop) % NZ
                ref = ring_ref(stream, place)
                if hop > 0:
                    wait_for(ref, ring_recv.at[stream, place])
                if hop < far(stream)[way]:
                    ring_copy(stream, ref, place, way, hop).start()

    def ring_sent(stream):
        for way in range(2):
            for hop in range(far(stream)[way]):
                place = (z - hop + NZ) % NZ if way == 0 else (z + hop) % NZ
                wait_for(ring_ref(stream, place), ring_send.at[stream, way, hop])

    def first_product(place):
        outer = lax.dot_general(
            a_own[...], a_ring[place], (((1,), (1,)), ((), ())),
            preferred_element_type=jnp.float32,
        )
        damped = BETA * f_work[place].astype(jnp.float32) + ((1.0 - BETA) / TOK) * outer
        total[...] += jnp.dot(
            damped.astype(jnp.bfloat16), w_ring[place], preferred_element_type=jnp.float32
        )

    def second_product(place):
        total[...] += jnp.dot(
            p_work[place], x_ring[place], preferred_element_type=jnp.float32
        )

    def both(product, hop):
        if hop == 0:
            product(z)
        elif hop == HOPS:
            product((z + HOPS) % NZ)
        else:
            def one(s, carry):
                product((z + NZ + (1 - 2 * s) * hop) % NZ)
                return carry
            lax.fori_loop(0, 2, one, 0)

    wait_for(w_ring.at[z, pl.ds(0, ROWS)], swap_recv.at[0])
    step(0, 0)
    for b in range(2):
        wait_for(a_own.at[pl.ds(b * ROWS, ROWS)], swap_recv.at[1 + b])
    mine = pl.ds(pl.multiple_of(core * ROWS, 16), ROWS)
    other = pl.ds(pl.multiple_of((1 - core) * ROWS, 16), ROWS)
    a_ring[z, 0:ROWS, :] = a_own[mine, :]
    step(1, 0)

    p_load.wait()
    relayout(p_in, p_out)
    send_panel(p_out, p_work, 5)

    total[...] = jnp.zeros_like(total)
    computed = 0
    for hop in range(1, HOPS + 1):
        step(0, hop)
        step(1, hop)
        if hop == 4:
            for b in range(2):
                wait_for(f_work.at[:, pl.ds(b * ROWS, ROWS)], swap_recv.at[3 + b])
        if hop >= 4:
            for _ in range(2):
                if computed <= hop:
                    both(first_product, computed)
                    computed += 1
    while computed <= HOPS:
        both(first_product, computed)
        computed += 1

    def pair_up(which):
        copy = pltpu.make_async_remote_copy(
            src_ref=total.at[other], dst_ref=sibling_part.at[which],
            send_sem=pair_send.at[which], recv_sem=pair_recv.at[which],
            device_id=sibling, device_id_type=MESH,
        )
        copy.start()
        copy.wait()

    @pl.when(jnp.logical_not(same))
    def _():
        wait_for(damp_in, swap_recv.at[7])

    pair_up(0)
    window = w_ring[z, 0:ROWS, :].astype(jnp.float32)
    applied = total[mine, :] + sibling_part[0] + damp_in[0:1, 0:1] * window
    x_ring[z, 0:ROWS, :] = applied.astype(jnp.bfloat16)
    step(2, 0)
    step(3, 0)
    total[...] = jnp.zeros_like(total)
    for b in range(2):
        wait_for(p_work.at[:, pl.ds(b * ROWS, ROWS)], swap_recv.at[5 + b])
    both(second_product, 0)
    for hop in range(1, HOPS + 1):
        step(2, hop)
        step(3, hop)
        both(second_product, hop)
    pair_up(1)
    fresh = 2.0 * window - (total[mine, :] + sibling_part[1])
    x_out = picked.at[0]
    x_out[0:ROWS, :] = fresh.astype(jnp.bfloat16)

    layer = chip * 2 + side
    for r in range(PIECES):
        target = 2 * r + r % 2
        deliver(
            x_out.at[pl.ds(r * 16, 16)], gathered.at[layer], give_send.at[r],
            give_recv.at[layer], (target, z * 2 + core),
            jnp.logical_and(slot == target, side == core),
        )

    piece = chip
    middle = jnp.logical_and(chip < PIECES, core == chip % 2)
    piece_rows = pl.ds(pl.multiple_of((chip % PIECES) * 16, 16), 16)

    @pl.when(middle)
    def _():
        for s in range(NS):
            wait_for(gathered.at[s], give_recv.at[s])
        for l in range(NS):
            picked[1, l * 16 : (l + 1) * 16, :] = gathered[owner[l]]
            deliver(
                picked.at[1, pl.ds(l * 16, 16)], out.at[0, piece_rows], pick_send.at[l],
                pick_recv.at[piece], (l, blk), slot == l,
            )

    for r in range(PIECES):
        wait_for(out.at[0, pl.ds(r * 16, 16)], pick_recv.at[r])

    sent(w_home, swap_send.at[0], same)
    for q in range(2):
        keep = jnp.logical_and(same, core == q)
        sent(a_home, swap_send.at[1 + q], keep)
        sent(f_out.at[q], swap_send.at[3 + q], keep)
        sent(p_out.at[q], swap_send.at[5 + q], keep)

    @pl.when(same)
    def _():
        wait_for(damp_out, swap_send.at[7])

    for stream in range(4):
        ring_sent(stream)
    for r in range(PIECES):
        sent(
            x_out.at[pl.ds(r * 16, 16)], give_send.at[r],
            jnp.logical_and(slot == 2 * r + r % 2, side == core),
        )

    @pl.when(middle)
    def _():
        for l in range(NS):
            sent(picked.at[1, pl.ds(l * 16, 16)], pick_send.at[l], slot == l)


def shards(owner, factor, inverse_old, acts_t, damping):
    bf16, f32 = jnp.bfloat16, jnp.float32
    dma = pltpu.SemaphoreType.DMA
    width = factor.shape[2]
    smem = pl.BlockSpec(memory_space=pltpu.SMEM)
    anywhere = pl.BlockSpec(memory_space=pl.ANY)
    return pl.pallas_call(
        kernel,
        out_shape=jax.ShapeDtypeStruct((1, ROWS, COLS), bf16),
        in_specs=[smem, smem, anywhere, anywhere, anywhere],
        out_specs=pl.BlockSpec(memory_space=pltpu.VMEM),
        scratch_shapes=[
            pltpu.VMEM((ROWS, width), f32),
            pltpu.VMEM((ROWS, width), bf16),
            pltpu.VMEM((2, NZ, ROWS, KP), bf16),
            pltpu.VMEM((2, NZ, ROWS, KP), bf16),
            pltpu.VMEM((NZ, 2 * ROWS, KP), bf16),
            pltpu.VMEM((NZ, 2 * ROWS, KP), bf16),
            pltpu.VMEM((2 * ROWS, TOK), bf16),
            pltpu.VMEM((NZ, KP, COLS), bf16),
            pltpu.VMEM((NZ, KP, TOK), bf16),
            pltpu.VMEM((NZ, KP, COLS), bf16),
            pltpu.VMEM((2 * ROWS, COLS), f32),
            pltpu.VMEM((2, ROWS, COLS), f32),
            pltpu.VMEM((8, 128), f32),
            pltpu.VMEM((8, 128), f32),
            pltpu.VMEM((NS, 16, COLS), bf16),
            pltpu.VMEM((2, 256, COLS), bf16),
            dma((2,)),
            dma((8,)),
            dma((8,)),
            dma((4, 2, HOPS)),
            dma((4, NZ)),
            dma((2,)),
            dma((2,)),
            dma((PIECES,)),
            dma((NS,)),
            dma((NS,)),
            dma((PIECES,)),
        ],
        compiler_params=pltpu.CompilerParams(
            collective_id=0, has_side_effects=True, vmem_limit_bytes=48 * 1024 * 1024
        ),
        cost_estimate=pl.CostEstimate(
            flops=2 * 3 * ROWS * width * COLS, bytes_accessed=3 * 1024 * 1024, transcendentals=0
        ),
    )(owner, damping, factor, inverse_old, acts_t)


def solution(mesh):
    placed = (
        P(),
        P("slot", "blk", None),
        P("slot", "blk", None),
        P("slot", "blk", None),
        P("slot"),
    )
    return jax.shard_map(
        shards, mesh=mesh, in_specs=placed, out_specs=P("slot", "blk", None), check_vma=False
    )
```

time: 520 us -> 126 us (0.24)
  waiting for transfers between devices: 487 us -> 0 us
  Pallas kernels: 0 us -> 120 us
  matrix products: 13.5 us -> 0 us
  between operations: 13.8 us -> 0.67 us
    all_gather x4 -> x0, waiting for transfers between devices: 486 us -> none  [the longest x1 140 us: shards(): lax.all_gather(applied, 'blk', axis=0, tiled=True)]
    pallas_call x0 -> x1, Pallas kernels: none -> 120 us  [shards(): pl.pallas_call(kernel, out_shape=jax.ShapeDtypeStruct((1, ROWS, COLS), bf...]
    dot_general x3 -> x0, matrix products: 13.5 us -> none  [the longest x1 5.23 us: shards(): jnp.dot(column_block, lax.all_gather(window, 'blk', axis=0, tiled=True).a...]
  transfers between devices with their start and end apart: 4 -> 0, of which waited for: 4 -> 0; matrix products, arithmetic and copies ran while one was open for 1% -> 0% of each run, Pallas kernels for 0% -> 0%
where the time goes in v1:
time: 126 us
  Pallas kernels  120 us (95%)
  local copies, waits for them, and re-layouts  4.78 us (4%)
    pallas_call x1, Pallas kernels, shards(): pl.pallas_call(kernel, out_shape=jax.ShapeDtypeStruct((1, ROWS, COLS), bf...  120 us
    unnamed x9, local copies, waits for them, and re-layouts  4.78 us

profile of v1, /device:TPU:1, one launch (start us, length us, event | category | flops | bytes accessed | tf_op | source)
XLA Modules:
  0.0 125.5 jit_solution(15773149770905135794)
XLA Ops:
  0.7 0.0 copy-start
  0.7 1.4 %copy-done = f32[1,112,3584]{2,1,0:T(8,128)S(1)} copy-done((f32[1,112,3584]{2,1,0:T(8,128)S(1)}, f32[1,112,3584]{2,1,0:T(8,128)}, u32[]{:S(2)}) %copy-start) | copy-done | bytes 1605656
  2.1 0.0 copy-start.1
  2.1 1.1 copy-done.1
  3.2 0.0 copy-start.2
  3.2 0.9 copy-done.2
  4.1 0.0 copy-start.3
  4.1 0.7 copy-done.3
  4.8 120.1 %shard_map.55 = bf16[1,112,640]{2,1,0:T(8,128)(2,1)S(1)} custom-call(s32[16]{0:T(128)S(1)} %copy-done.3, f32[1]{0:T(128)S(6)} %copy.7.damping, f32[1,112,3584]{2,1,0:T(8,128)S(1)} %copy-done, bf16[1,112,3584]{2,1,0:T(8,128)(2,1)S(1)} %copy-done.1, bf16[1,112,640]{2,1,0:T(8,128)(2,1)S(1)} %copy-done.2), custom_call_target="tpu_custom_call" | custom-call | flops 1541406720 | bytes 3145728 | tf_op jit(solution)/shard_map/pallas_call | solution.py:327
  124.9 0.7 copy.8
Async XLA Ops:
  0.7 1.4 %copy-start = (f32[1,112,3584]{2,1,0:T(8,128)S(1)}, f32[1,112,3584]{2,1,0:T(8,128)}, u32[]{:S(2)}) copy-start(f32[1,112,3584]{2,1,0:T(8,128)} %factor.1) | copy-start | bytes 4816900
  2.1 1.1 copy-start.1
  3.2 0.9 copy-start.2
  4.1 0.7 copy-start.3

commit v2 on v1

v2 whole, which is shorter than its diff:
```python
import jax
import jax.numpy as jnp
from jax import lax
from jax.experimental import pallas as pl
from jax.experimental.pallas import tpu as pltpu
from jax.sharding import PartitionSpec as P

COLS = 640
TOK = 640
BETA = 0.75
NZ = 16
NS = 16
ROWS = 112
KP = 128
PIECES = 7
MESH = pl.DeviceIdType.MESH
HOPS = NZ // 2
PARTS = (384, 256)
FIRST = (0, 384)
STREAMS = ((128, 128, 128), (128, 128))
LONG_UP = (0, 3, 4, 6, 7)


def wait_for(ref, sem):
    pltpu.make_async_copy(ref, ref, sem).wait()


def kernel(
    owner_home, damping, factor, inverse, acts, out,
    owner, f_in, p_in, f_out, p_out, f_work, p_work, a_own, a_ring,
    w_ring, x_ring, total, sibling_part, fresh, gathered, picked,
    damp_out, damp_in, load_sem,
    swap_send, swap_recv, ring_send, ring_recv, pair_send, pair_recv,
    give_send, give_recv, pick_send, pick_recv, hello,
):
    slot = lax.axis_index("slot")
    blk = lax.axis_index("blk")
    chip = slot // 2
    core = slot % 2
    z = blk // 2
    side = blk % 2
    same = core == side

    def at(core_at, side_at, z_at):
        return (chip * 2 + core_at, z_at * 2 + side_at)

    sibling = at(1 - core, side, z)
    up = at(core, side, (z + 1) % NZ)
    down = at(core, side, (z + NZ - 1) % NZ)

    f_load = pltpu.make_async_copy(factor.at[0], f_in, load_sem.at[0])
    p_load = pltpu.make_async_copy(inverse.at[0], p_in, load_sem.at[1])
    f_load.start()
    p_load.start()
    owner_load = pltpu.make_async_copy(owner_home, owner, load_sem.at[2])
    owner_load.start()

    barrier = pltpu.get_barrier_semaphore()
    flips = [((chip + 4) % 8, core), (chip // 2 * 2 + 1 - chip % 2, core),
             (chip // 4 * 4 + (chip % 4 + 2) % 4, core)]
    partners = [up, down, sibling, at(core, 1 - side, z), at(1 - core, 1 - side, z)]
    far_partners = [(c * 2 + k, blk) for c, k in flips]
    for target in partners + far_partners:
        pl.semaphore_signal(barrier, inc=1, device_id=target, device_id_type=MESH)

    def greet(i):
        pl.semaphore_signal(
            hello.at[i], inc=1, device_id=far_partners[i], device_id_type=MESH
        )

    def greeted(i):
        pl.semaphore_wait(hello.at[i], 1)

    pad = jnp.zeros((KP - ROWS, COLS), jnp.bfloat16)

    def clear(i, carry):
        for p in range(2):
            a_ring[p][i, ROWS:KP, :] = pad[:, : PARTS[p]]
            w_ring[p][i, ROWS:KP, :] = pad[:, : PARTS[p]]
            for q, width in enumerate(STREAMS[p]):
                x_ring[p][q][i, ROWS:KP, :] = pad[:, :width]
        return carry

    lax.fori_loop(0, NZ, clear, 0)
    def relayout(src, dst):
        for j in range(2 * NZ):
            start = ROWS * j
            base = start // 128 * 128
            off = start - base
            if off == 0:
                piece = src[:, base : base + 128].astype(jnp.bfloat16)
            elif off + ROWS <= 128:
                piece = pltpu.roll(
                    src[:, base : base + 128].astype(jnp.float32), 128 - off, 1
                ).astype(jnp.bfloat16)
            else:
                piece = pltpu.roll(
                    src[:, base : base + 256].astype(jnp.float32), 256 - off, 1
                )[:, :128].astype(jnp.bfloat16)
            dst[j % 2, j // 2] = piece

    pl.semaphore_wait(barrier, len(partners) + len(far_partners))
    greet(0)

    pending = []

    def deliver(src, dst, send, recv, target, own):
        pending.append(lambda: sent(src, send, own))

        @pl.when(own)
        def _():
            pltpu.make_async_copy(src, dst, recv).start()

        @pl.when(jnp.logical_not(own))
        def _():
            pltpu.make_async_remote_copy(
                src_ref=src, dst_ref=dst, send_sem=send, recv_sem=recv,
                device_id=target, device_id_type=MESH,
            ).start()

    def sent(src, send, own):
        @pl.when(jnp.logical_not(own))
        def _():
            wait_for(src, send)

    w_home = [inverse.at[0, :, pl.ds(FIRST[p], PARTS[p])] for p in range(2)]
    a_home = acts.at[0]
    for p in range(2):
        deliver(
            w_home[p], w_ring[p].at[z, pl.ds(0, ROWS)], swap_send.at[8 * p],
            swap_recv.at[8 * p], at(side, core, z), same,
        )
    own_rows = pl.ds(pl.multiple_of(side * ROWS, 16), ROWS)
    for q in range(2):
        deliver(
            a_home, a_own.at[own_rows], swap_send.at[1 + q], swap_recv.at[1 + side],
            at(q, core, z), jnp.logical_and(same, core == q),
        )

    damp_out[...] = jnp.full((8, 128), damping[0], jnp.float32)

    @pl.when(same)
    def _():
        damp_in[...] = damp_out[...]
        pltpu.make_async_remote_copy(
            src_ref=damp_out, dst_ref=damp_in, send_sem=swap_send.at[7],
            recv_sem=swap_recv.at[7], device_id=sibling, device_id_type=MESH,
        ).start()

    def send_panel(src, dst, first):
        for q in range(2):
            deliver(
                src.at[q], dst.at[:, own_rows], swap_send.at[first + q],
                swap_recv.at[first + side],
                at(q, core, z), jnp.logical_and(same, core == q),
            )

    rings = [a_ring[0], a_ring[1], w_ring[0], w_ring[1]]
    streams_of = []
    for p in range(2):
        streams_of.append(range(len(rings), len(rings) + len(STREAMS[p])))
        rings += [x_ring[p][q] for q in range(len(STREAMS[p]))]

    def ring_ref(stream, place):
        return rings[stream].at[place, pl.ds(0, ROWS)]

    def far(stream):
        return (HOPS, HOPS - 1) if stream in LONG_UP else (HOPS - 1, HOPS)

    def place_of(way, hop):
        return (z - hop + NZ) % NZ if way == 0 else (z + hop) % NZ

    def step(stream, hop):
        for way in range(2):
            if hop <= far(stream)[way]:
                place = place_of(way, hop)
                ref = ring_ref(stream, place)
                if hop > 0:
                    wait_for(ref, ring_recv.at[stream, place])
                if hop < far(stream)[way]:
                    pltpu.make_async_remote_copy(
                        src_ref=ref, dst_ref=ref, send_sem=ring_send.at[stream, way, hop],
                        recv_sem=ring_recv.at[stream, place],
                        device_id=up if way == 0 else down, device_id_type=MESH,
                    ).start()
                    pending.append(
                        lambda r=ref, m=ring_send.at[stream, way, hop]: wait_for(r, m)
                    )

    def damp_block(place):
        outer = sum(
            lax.dot_general(
                a_own[:, FIRST[p] : FIRST[p] + PARTS[p]], a_ring[p][place],
                (((1,), (1,)), ((), ())), preferred_element_type=jnp.float32,
            )
            for p in range(2)
        )
        damped = BETA * f_work[place].astype(jnp.float32) + ((1.0 - BETA) / TOK) * outer
        f_work[place] = damped.astype(jnp.bfloat16)

    def first_product(p):
        def product(place):
            total[p][...] += jnp.dot(
                f_work[place], w_ring[p][place], preferred_element_type=jnp.float32
            )
        return product

    def second_product(p):
        def product(place):
            first = 0
            for q, width in enumerate(STREAMS[p]):
                total[p][:, first : first + width] += jnp.dot(
                    p_work[place], x_ring[p][q][place], preferred_element_type=jnp.float32
                )
                first += width
        return product

    def both(product, hop):
        if hop == 0:
            product(z)
        elif hop == HOPS:
            product((z + HOPS) % NZ)
        else:
            def one(s, carry):
                product((z + NZ + (1 - 2 * s) * hop) % NZ)
                return carry
            lax.fori_loop(0, 2, one, 0)

    mine = pl.ds(pl.multiple_of(core * ROWS, 16), ROWS)
    other = pl.ds(pl.multiple_of((1 - core) * ROWS, 16), ROWS)

    def pair_copy(p, phase):
        return pltpu.make_async_remote_copy(
            src_ref=total[p].at[other], dst_ref=sibling_part[p].at[phase],
            send_sem=pair_send.at[p, phase], recv_sem=pair_recv.at[p, phase],
            device_id=sibling, device_id_type=MESH,
        )

    for p in range(2):
        wait_for(w_ring[p].at[z, pl.ds(0, ROWS)], swap_recv.at[8 * p])
        step(2 + p, 0)
    wait_for(a_own.at[mine], swap_recv.at[1 + core])
    first = 0
    for p in range(2):
        a_ring[p][z, 0:ROWS, :] = a_own[mine, first : first + PARTS[p]]
        first += PARTS[p]
        step(p, 0)
    f_load.wait()
    relayout(f_in, f_out)
    wait_for(a_own.at[other], swap_recv.at[2 - core])
    send_panel(f_out, f_work, 3)
    p_load.wait()
    owner_load.wait()
    relayout(p_in, p_out)
    for p in range(2):
        total[p][...] = jnp.zeros_like(total[p])

    done = [0, 0]

    def catch_up(p, hop):
        for _ in range(2):
            if done[p] <= hop:
                if p == 0:
                    both(damp_block, done[p])
                both(first_product(p), done[p])
                done[p] += 1

    for hop in range(1, HOPS + 1):
        for stream in range(3):
            step(stream, hop)
        if hop < HOPS:
            step(3, hop)
        if hop in (2, 4, 6):
            greeted(hop // 2 - 1)
            if hop < 6:
                greet(hop // 2)
        if hop == 4:
            for b in range(2):
                wait_for(f_work.at[:, pl.ds(b * ROWS, ROWS)], swap_recv.at[3 + b])
            send_panel(p_out, p_work, 5)
        if hop >= 4:
            catch_up(0, hop)
            if hop == HOPS:
                pair_copy(0, 0).start()
                step(3, hop)
            catch_up(1, hop)

    @pl.when(jnp.logical_not(same))
    def _():
        wait_for(damp_in, swap_recv.at[7])

    def apply(p):
        pair_copy(p, 0).wait()
        window = w_ring[p][z, 0:ROWS, :].astype(jnp.float32)
        applied = total[p][mine, :] + sibling_part[p][0] + damp_in[0:1, 0:1] * window
        applied = applied.astype(jnp.bfloat16)
        first = 0
        for q, width in enumerate(STREAMS[p]):
            x_ring[p][q][z, 0:ROWS, :] = applied[:, first : first + width]
            step(streams_of[p][q], 0)
            first += width
        total[p][...] = jnp.zeros_like(total[p])

    pair_copy(1, 0).start()
    apply(0)
    apply(1)
    for b in range(2):
        wait_for(p_work.at[:, pl.ds(b * ROWS, ROWS)], swap_recv.at[5 + b])
    for p in range(2):
        both(second_product(p), 0)
    for hop in range(1, HOPS + 1):
        for p in range(2):
            for stream in streams_of[p]:
                step(stream, hop)
            both(second_product(p), hop)
            if hop == HOPS:
                pair_copy(p, 1).start()

    layer = chip * 2 + side
    for p in range(2):
        pair_copy(p, 1).wait()
        window = w_ring[p][z, 0:ROWS, :].astype(jnp.float32)
        fresh[p][...] = (
            2.0 * window - (total[p][mine, :] + sibling_part[p][1])
        ).astype(jnp.bfloat16)
        for r in range(PIECES):
            target = 2 * r + r % 2
            deliver(
                fresh[p].at[pl.ds(r * 16, 16)], gathered[p].at[layer],
                give_send.at[p, r], give_recv.at[p, layer], (target, z * 2 + core),
                jnp.logical_and(slot == target, side == core),
            )

    piece = chip
    middle = jnp.logical_and(chip < PIECES, core == chip % 2)
    piece_rows = pl.ds(pl.multiple_of((chip % PIECES) * 16, 16), 16)

    @pl.when(middle)
    def _():
        for p in range(2):
            for s in range(NS):
                wait_for(gathered[p].at[s], give_recv.at[p, s])
            for l in range(NS):
                picked[p][l * 16 : (l + 1) * 16, :] = gathered[p][owner[l]]
                deliver(
                    picked[p].at[pl.ds(l * 16, 16)],
                    out.at[0, piece_rows, pl.ds(FIRST[p], PARTS[p])],
                    pick_send.at[p, l], pick_recv.at[p, piece], (l, blk), slot == l,
                )
                pending.pop()

    for left in pending:
        left()

    @pl.when(same)
    def _():
        wait_for(damp_out, swap_send.at[7])

    @pl.when(middle)
    def _():
        for p in range(2):
            for l in range(NS):
                sent(picked[p].at[pl.ds(l * 16, 16)], pick_send.at[p, l], slot == l)

    for p in range(2):
        for r in range(PIECES):
            wait_for(
                out.at[0, pl.ds(r * 16, 16), pl.ds(FIRST[p], PARTS[p])], pick_recv.at[p, r]
            )


def shards(owner, factor, inverse_old, acts_t, damping):
    bf16, f32 = jnp.bfloat16, jnp.float32
    dma, vmem = pltpu.SemaphoreType.DMA, pltpu.VMEM
    n_streams = 4 + sum(len(widths) for widths in STREAMS)
    width = factor.shape[2]
    smem = pl.BlockSpec(memory_space=pltpu.SMEM)
    anywhere = pl.BlockSpec(memory_space=pltpu.HBM)
    return pl.pallas_call(
        kernel,
        out_shape=jax.ShapeDtypeStruct((1, ROWS, COLS), bf16),
        in_specs=[anywhere, smem, anywhere, anywhere, anywhere],
        out_specs=pl.BlockSpec(memory_space=pltpu.VMEM),
        scratch_shapes=[
            pltpu.SMEM((NS,), jnp.int32),
            vmem((ROWS, width), f32),
            vmem((ROWS, width), bf16),
            vmem((2, NZ, ROWS, KP), bf16),
            vmem((2, NZ, ROWS, KP), bf16),
            vmem((NZ, 2 * ROWS, KP), bf16),
            vmem((NZ, 2 * ROWS, KP), bf16),
            vmem((2 * ROWS, TOK), bf16),
            [vmem((NZ, KP, n), bf16) for n in PARTS],
            [vmem((NZ, KP, n), bf16) for n in PARTS],
            [[vmem((NZ, KP, n), bf16) for n in widths] for widths in STREAMS],
            [vmem((2 * ROWS, n), f32) for n in PARTS],
            [vmem((2, ROWS, n), f32) for n in PARTS],
            [vmem((ROWS, n), bf16) for n in PARTS],
            [vmem((NS, 16, n), bf16) for n in PARTS],
            [vmem((NS * 16, n), bf16) for n in PARTS],
            vmem((8, 128), f32),
            vmem((8, 128), f32),
            dma((3,)),
            dma((9,)),
            dma((9,)),
            dma((n_streams, 2, HOPS)),
            dma((n_streams, NZ)),
            dma((2, 2)),
            dma((2, 2)),
            dma((2, PIECES)),
            dma((2, NS)),
            dma((2, NS)),
            dma((2, PIECES)),
            pltpu.SemaphoreType.REGULAR((3,)),
        ],
        compiler_params=pltpu.CompilerParams(
            collective_id=0, has_side_effects=True, vmem_limit_bytes=60 * 1024 * 1024
        ),
        cost_estimate=pl.CostEstimate(
            flops=2 * 3 * ROWS * width * COLS, bytes_accessed=3 * 1024 * 1024, transcendentals=0
        ),
    )(owner, damping, factor, inverse_old, acts_t)


def solution(mesh):
    placed = (
        P(),
        P("slot", "blk", None),
        P("slot", "blk", None),
        P("slot", "blk", None),
        P("slot"),
    )
    return jax.shard_map(
        shards, mesh=mesh, in_specs=placed, out_specs=P("slot", "blk", None), check_vma=False
    )
```

time: 126 us -> 114 us (0.905)
  Pallas kernels: 120 us -> 112 us
  local copies, waits for them, and re-layouts: 4.78 us -> 1.58 us
    pallas_call x1, Pallas kernels: 120 us -> 112 us  [shards(): pl.pallas_call(kernel, out_shape=jax.ShapeDtypeStruct((1, ROWS, COLS), bf...]
    unnamed x9 -> x1, local copies, waits for them, and re-layouts: 4.78 us -> 1.58 us
where the time goes in v2:
time: 114 us
  Pallas kernels  112 us (98%)
  local copies, waits for them, and re-layouts  1.58 us (1%)
    pallas_call x1, Pallas kernels, shards(): pl.pallas_call(kernel, out_shape=jax.ShapeDtypeStruct((1, ROWS, COLS), bf...  112 us

profile of v2, /device:TPU:1, one launch (start us, length us, event | category | flops | bytes accessed | tf_op | source)
XLA Modules:
  0.0 114.3 jit_solution(12483789566108549549)
XLA Ops:
  0.7 112.0 %shard_map.55 = bf16[1,112,640]{2,1,0:T(8,128)(2,1)} custom-call(s32[16]{0:T(128)} %owner_home.1, f32[1]{0:T(128)S(6)} %copy.7.damping, f32[1,112,3584]{2,1,0:T(8,128)} %factor.1, bf16[1,112,3584]{2,1,0:T(8,128)(2,1)} %inverse.1, bf16[1,112,640]{2,1,0:T(8,128)(2,1)} %acts.1), custom_call_target="tpu_custom_call" | custom-call | flops 1541406720 | bytes 3145728 | tf_op jit(solution)/shard_map/pallas_call | solution.py:379
  112.7 1.6 %copy.8 = bf16[1,112,640]{2,1,0:T(8,128)(2,1)} copy(bf16[1,112,640]{2,1,0:T(8,128)(2,1)} %shard_map.55) | data formatting | bytes 286720

commit v3 on v2

--- a/solution.py
+++ b/solution.py
@@ -15,10 +15,10 @@
 PIECES = 7
 MESH = pl.DeviceIdType.MESH
 HOPS = NZ // 2
-PARTS = (384, 256)
-FIRST = (0, 384)
-STREAMS = ((128, 128, 128), (128, 128))
-LONG_UP = (0, 3, 4, 6, 7)
+PARTS = (256, 384)
+FIRST = (0, 256)
+STREAMS = ((128, 128), (128, 128, 128))
+LONG_UP = (0, 3, 4, 6, 8)
 
 
 def wait_for(ref, sem):
@@ -48,6 +48,20 @@
     up = at(core, side, (z + 1) % NZ)
     down = at(core, side, (z + NZ - 1) % NZ)
 
+    barrier = pltpu.get_barrier_semaphore()
+    def other_chip(c, side_at):
+        return (c * 2 + core, z * 2 + side_at)
+
+    along_x = chip // 4 * 4
+    far_partners = [
+        other_chip((chip + 4) % 8, 1 - side),
+        other_chip(along_x + chip % 4 // 2 * 2 + 1 - chip % 2, side),
+        other_chip(along_x + 3 - chip % 4, side),
+    ]
+    partners = [up, down, sibling, at(core, 1 - side, z), at(1 - core, 1 - side, z)]
+    for target in partners + far_partners:
+        pl.semaphore_signal(barrier, inc=1, device_id=target, device_id_type=MESH)
+
     f_load = pltpu.make_async_copy(factor.at[0], f_in, load_sem.at[0])
     p_load = pltpu.make_async_copy(inverse.at[0], p_in, load_sem.at[1])
     f_load.start()
@@ -55,14 +69,6 @@
     owner_load = pltpu.make_async_copy(owner_home, owner, load_sem.at[2])
     owner_load.start()
 
-    barrier = pltpu.get_barrier_semaphore()
-    flips = [((chip + 4) % 8, core), (chip // 2 * 2 + 1 - chip % 2, core),
-             (chip // 4 * 4 + (chip % 4 + 2) % 4, core)]
-    partners = [up, down, sibling, at(core, 1 - side, z), at(1 - core, 1 - side, z)]
-    far_partners = [(c * 2 + k, blk) for c, k in flips]
-    for target in partners + far_partners:
-        pl.semaphore_signal(barrier, inc=1, device_id=target, device_id_type=MESH)
-
     def greet(i):
         pl.semaphore_signal(
             hello.at[i], inc=1, device_id=far_partners[i], device_id_type=MESH
@@ -70,6 +76,39 @@
 
     def greeted(i):
         pl.semaphore_wait(hello.at[i], 1)
+
+    pending = []
+
+    def keep(src, dst, recv, own):
+        @pl.when(own)
+        def _():
+            pltpu.make_async_copy(src, dst, recv).start()
+
+    def deliver(src, dst, send, recv, target, own, kept=False):
+        pending.append(lambda: sent(src, send, own))
+
+        if not kept:
+            keep(src, dst, recv, own)
+
+        @pl.when(jnp.logical_not(own))
+        def _():
+            pltpu.make_async_remote_copy(
+                src_ref=src, dst_ref=dst, send_sem=send, recv_sem=recv,
+                device_id=target, device_id_type=MESH,
+            ).start()
+
+    def sent(src, send, own):
+        @pl.when(jnp.logical_not(own))
+        def _():
+            wait_for(src, send)
+
+    w_home = [inverse.at[0, :, pl.ds(FIRST[p], PARTS[p])] for p in range(2)]
+    a_home = acts.at[0]
+    own_rows = pl.ds(pl.multiple_of(side * ROWS, 16), ROWS)
+
+    for p in range(2):
+        keep(w_home[p], w_ring[p].at[z, pl.ds(0, ROWS)], swap_recv.at[8 * p], same)
+    keep(a_home, a_own.at[own_rows], swap_recv.at[1 + side], same)
 
     pad = jnp.zeros((KP - ROWS, COLS), jnp.bfloat16)
 
@@ -102,40 +141,22 @@
     pl.semaphore_wait(barrier, len(partners) + len(far_partners))
     greet(0)
 
-    pending = []
-
-    def deliver(src, dst, send, recv, target, own):
-        pending.append(lambda: sent(src, send, own))
-
-        @pl.when(own)
-        def _():
-            pltpu.make_async_copy(src, dst, recv).start()
-
-        @pl.when(jnp.logical_not(own))
-        def _():
-            pltpu.make_async_remote_copy(
-                src_ref=src, dst_ref=dst, send_sem=send, recv_sem=recv,
-                device_id=target, device_id_type=MESH,
-            ).start()
-
-    def sent(src, send, own):
-        @pl.when(jnp.logical_not(own))
-        def _():
-            wait_for(src, send)
-
-    w_home = [inverse.at[0, :, pl.ds(FIRST[p], PARTS[p])] for p in range(2)]
-    a_home = acts.at[0]
-    for p in range(2):
+    def swap_w(p):
         deliver(
             w_home[p], w_ring[p].at[z, pl.ds(0, ROWS)], swap_send.at[8 * p],
-            swap_recv.at[8 * p], at(side, core, z), same,
+            swap_recv.at[8 * p], at(side, core, z), same, True,
         )
-    own_rows = pl.ds(pl.multiple_of(side * ROWS, 16), ROWS)
-    for q in range(2):
+
+    def swap_a(q, own):
         deliver(
             a_home, a_own.at[own_rows], swap_send.at[1 + q], swap_recv.at[1 + side],
-            at(q, core, z), jnp.logical_and(same, core == q),
+            at(side if q == 0 else 1 - side, core, z), own, True,
         )
+
+    swap_w(0)
+    swap_a(0, same)
+    swap_w(1)
+    swap_a(1, False)
 
     damp_out[...] = jnp.full((8, 128), damping[0], jnp.float32)
 
@@ -236,15 +257,16 @@
             device_id=sibling, device_id_type=MESH,
         )
 
-    for p in range(2):
-        wait_for(w_ring[p].at[z, pl.ds(0, ROWS)], swap_recv.at[8 * p])
-        step(2 + p, 0)
+    wait_for(w_ring[0].at[z, pl.ds(0, ROWS)], swap_recv.at[0])
+    step(2, 0)
     wait_for(a_own.at[mine], swap_recv.at[1 + core])
     first = 0
     for p in range(2):
         a_ring[p][z, 0:ROWS, :] = a_own[mine, first : first + PARTS[p]]
         first += PARTS[p]
         step(p, 0)
+    wait_for(w_ring[1].at[z, pl.ds(0, ROWS)], swap_recv.at[8])
+    step(3, 0)
     f_load.wait()
     relayout(f_in, f_out)
     wait_for(a_own.at[other], swap_recv.at[2 - core])
@@ -266,7 +288,7 @@
                 done[p] += 1
 
     for hop in range(1, HOPS + 1):
-        for stream in range(3):
+        for stream in (2, 0, 1):
             step(stream, hop)
         if hop < HOPS:
             step(3, hop)
@@ -312,9 +334,12 @@
         for p in range(2):
             for stream in streams_of[p]:
                 step(stream, hop)
-            both(second_product(p), hop)
             if hop == HOPS:
+                both(second_product(p), hop)
                 pair_copy(p, 1).start()
+        if hop < HOPS:
+            for p in range(2):
+                both(second_product(p), hop)
 
     layer = chip * 2 + side
     for p in range(2):
@@ -324,28 +349,28 @@
             2.0 * window - (total[p][mine, :] + sibling_part[p][1])
         ).astype(jnp.bfloat16)
         for r in range(PIECES):
-            target = 2 * r + r % 2
+            target = 2 * r + p
             deliver(
                 fresh[p].at[pl.ds(r * 16, 16)], gathered[p].at[layer],
                 give_send.at[p, r], give_recv.at[p, layer], (target, z * 2 + core),
                 jnp.logical_and(slot == target, side == core),
             )
 
-    piece = chip
-    middle = jnp.logical_and(chip < PIECES, core == chip % 2)
+    def middle(p):
+        return jnp.logical_and(chip < PIECES, core == p)
+
     piece_rows = pl.ds(pl.multiple_of((chip % PIECES) * 16, 16), 16)
-
-    @pl.when(middle)
-    def _():
-        for p in range(2):
-            for s in range(NS):
-                wait_for(gathered[p].at[s], give_recv.at[p, s])
+    for p in range(2):
+        @pl.when(middle(p))
+        def _():
+            for layer_at in range(NS):
+                wait_for(gathered[p].at[layer_at], give_recv.at[p, layer_at])
             for l in range(NS):
                 picked[p][l * 16 : (l + 1) * 16, :] = gathered[p][owner[l]]
                 deliver(
                     picked[p].at[pl.ds(l * 16, 16)],
                     out.at[0, piece_rows, pl.ds(FIRST[p], PARTS[p])],
-                    pick_send.at[p, l], pick_recv.at[p, piece], (l, blk), slot == l,
+                    pick_send.at[p, l], pick_recv.at[p, chip], (l, blk), slot == l,
                 )
                 pending.pop()
 
@@ -356,9 +381,9 @@
     def _():
         wait_for(damp_out, swap_send.at[7])
 
-    @pl.when(middle)
-    def _():
-        for p in range(2):
+    for p in range(2):
+        @pl.when(middle(p))
+        def _():
             for l in range(NS):
                 sent(picked[p].at[pl.ds(l * 16, 16)], pick_send.at[p, l], slot == l)
 
@@ -380,7 +405,7 @@
         kernel,
         out_shape=jax.ShapeDtypeStruct((1, ROWS, COLS), bf16),
         in_specs=[anywhere, smem, anywhere, anywhere, anywhere],
-        out_specs=pl.BlockSpec(memory_space=pltpu.VMEM),
+        out_specs=anywhere,
         scratch_shapes=[
             pltpu.SMEM((NS,), jnp.int32),
             vmem((ROWS, width), f32),

time: 114 us -> 111 us (0.974)
  Pallas kernels: 112 us -> 108 us
    pallas_call x1, Pallas kernels: 112 us -> 108 us  [shards(): pl.pallas_call(kernel, out_shape=jax.ShapeDtypeStruct((1, ROWS, COLS), bf...]
where the time goes in v3:
time: 111 us
  Pallas kernels  108 us (97%)
  local copies, waits for them, and re-layouts  1.58 us (1%)
    pallas_call x1, Pallas kernels, shards(): pl.pallas_call(kernel, out_shape=jax.ShapeDtypeStruct((1, ROWS, COLS), bf...  108 us

profile of v3, /device:TPU:1, one launch (start us, length us, event | category | flops | bytes accessed | tf_op | source)
XLA Modules:
  0.0 110.7 jit_solution(15212488558511751119)
XLA Ops:
  0.7 108.4 %shard_map.55 = bf16[1,112,640]{2,1,0:T(8,128)(2,1)} custom-call(s32[16]{0:T(128)} %owner_home.1, f32[1]{0:T(128)S(6)} %copy.7.damping, f32[1,112,3584]{2,1,0:T(8,128)} %factor.1, bf16[1,112,3584]{2,1,0:T(8,128)(2,1)} %inverse.1, bf16[1,112,640]{2,1,0:T(8,128)(2,1)} %acts.1), custom_call_target="tpu_custom_call" | custom-call | flops 1541406720 | bytes 3145728 | tf_op jit(solution)/shard_map/pallas_call | solution.py:404
  109.1 1.6 %copy.8 = bf16[1,112,640]{2,1,0:T(8,128)(2,1)} copy(bf16[1,112,640]{2,1,0:T(8,128)(2,1)} %shard_map.55) | data formatting | bytes 286720

commit v4 on v3

--- a/solution.py
+++ b/solution.py
@@ -59,6 +59,14 @@
         other_chip(along_x + 3 - chip % 4, side),
     ]
     partners = [up, down, sibling, at(core, 1 - side, z), at(1 - core, 1 - side, z)]
+    swap_up = at(side, core, (z + 1) % NZ)
+    swap_down = at(side, core, (z + NZ - 1) % NZ)
+
+    @pl.when(jnp.logical_not(same))
+    def _():
+        for target in (swap_up, swap_down):
+            pl.semaphore_signal(barrier, inc=1, device_id=target, device_id_type=MESH)
+
     for target in partners + far_partners:
         pl.semaphore_signal(barrier, inc=1, device_id=target, device_id_type=MESH)
 
@@ -138,7 +146,14 @@
                 )[:, :128].astype(jnp.bfloat16)
             dst[j % 2, j // 2] = piece
 
-    pl.semaphore_wait(barrier, len(partners) + len(far_partners))
+    @pl.when(same)
+    def _():
+        pl.semaphore_wait(barrier, len(partners) + len(far_partners))
+
+    @pl.when(jnp.logical_not(same))
+    def _():
+        pl.semaphore_wait(barrier, len(partners) + len(far_partners) + 2)
+
     greet(0)
 
     def swap_w(p):
@@ -153,6 +168,36 @@
             at(side if q == 0 else 1 - side, core, z), own, True,
         )
 
+    rings = [a_ring[0], a_ring[1], w_ring[0], w_ring[1]]
+    streams_of = []
+    for p in range(2):
+        streams_of.append(range(len(rings), len(rings) + len(STREAMS[p])))
+        rings += [x_ring[p][q] for q in range(len(STREAMS[p]))]
+
+    def ring_ref(stream, place):
+        return rings[stream].at[place, pl.ds(0, ROWS)]
+
+    def far(stream):
+        return (HOPS, HOPS - 1) if stream in LONG_UP else (HOPS - 1, HOPS)
+
+    def place_of(way, hop):
+        return (z - hop + NZ) % NZ if way == 0 else (z + hop) % NZ
+
+    def first_hop(stream):
+        p = stream % 2
+        home = w_home[p] if stream >= 2 else a_home.at[:, pl.ds(FIRST[p], PARTS[p])]
+        for way in range(2):
+            pltpu.make_async_remote_copy(
+                src_ref=home, dst_ref=ring_ref(stream, z),
+                send_sem=ring_send.at[stream, way, 0], recv_sem=ring_recv.at[stream, z],
+                device_id=swap_up if way == 0 else swap_down, device_id_type=MESH,
+            ).start()
+            pending.append(lambda r=home, m=ring_send.at[stream, way, 0]: wait_for(r, m))
+
+    first_hop(2)
+    first_hop(0)
+    first_hop(1)
+    first_hop(3)
     swap_w(0)
     swap_a(0, same)
     swap_w(1)
@@ -175,21 +220,6 @@
                 swap_recv.at[first + side],
                 at(q, core, z), jnp.logical_and(same, core == q),
             )
-
-    rings = [a_ring[0], a_ring[1], w_ring[0], w_ring[1]]
-    streams_of = []
-    for p in range(2):
-        streams_of.append(range(len(rings), len(rings) + len(STREAMS[p])))
-        rings += [x_ring[p][q] for q in range(len(STREAMS[p]))]
-
-    def ring_ref(stream, place):
-        return rings[stream].at[place, pl.ds(0, ROWS)]
-
-    def far(stream):
-        return (HOPS, HOPS - 1) if stream in LONG_UP else (HOPS - 1, HOPS)
-
-    def place_of(way, hop):
-        return (z - hop + NZ) % NZ if way == 0 else (z + hop) % NZ
 
     def step(stream, hop):
         for way in range(2):
@@ -257,19 +287,8 @@
             device_id=sibling, device_id_type=MESH,
         )
 
-    wait_for(w_ring[0].at[z, pl.ds(0, ROWS)], swap_recv.at[0])
-    step(2, 0)
-    wait_for(a_own.at[mine], swap_recv.at[1 + core])
-    first = 0
-    for p in range(2):
-        a_ring[p][z, 0:ROWS, :] = a_own[mine, first : first + PARTS[p]]
-        first += PARTS[p]
-        step(p, 0)
-    wait_for(w_ring[1].at[z, pl.ds(0, ROWS)], swap_recv.at[8])
-    step(3, 0)
     f_load.wait()
     relayout(f_in, f_out)
-    wait_for(a_own.at[other], swap_recv.at[2 - core])
     send_panel(f_out, f_work, 3)
     p_load.wait()
     owner_load.wait()
@@ -296,9 +315,16 @@
             greeted(hop // 2 - 1)
             if hop < 6:
                 greet(hop // 2)
+        if hop == 2:
+            for p in range(2):
+                wait_for(w_ring[p].at[z, pl.ds(0, ROWS)], swap_recv.at[8 * p])
+            wait_for(a_own.at[mine], swap_recv.at[1 + core])
+            for p in range(2):
+                a_ring[p][z, 0:ROWS, :] = a_own[mine, FIRST[p] : FIRST[p] + PARTS[p]]
         if hop == 4:
             for b in range(2):
                 wait_for(f_work.at[:, pl.ds(b * ROWS, ROWS)], swap_recv.at[3 + b])
+            wait_for(a_own.at[other], swap_recv.at[2 - core])
             send_panel(p_out, p_work, 5)
         if hop >= 4:
             catch_up(0, hop)
@@ -330,6 +356,7 @@
         wait_for(p_work.at[:, pl.ds(b * ROWS, ROWS)], swap_recv.at[5 + b])
     for p in range(2):
         both(second_product(p), 0)
+    early, pending[:] = list(pending), []
     for hop in range(1, HOPS + 1):
         for p in range(2):
             for stream in streams_of[p]:
@@ -340,6 +367,8 @@
         if hop < HOPS:
             for p in range(2):
                 both(second_product(p), hop)
+        for left in early[(hop - 1) * len(early) // 6 : hop * len(early) // 6]:
+            left()
 
     layer = chip * 2 + side
     for p in range(2):
@@ -355,6 +384,10 @@
                 give_send.at[p, r], give_recv.at[p, layer], (target, z * 2 + core),
                 jnp.logical_and(slot == target, side == core),
             )
+
+    for left in pending[:-2 * PIECES]:
+        left()
+    pending[:] = pending[-2 * PIECES :]
 
     def middle(p):
         return jnp.logical_and(chip < PIECES, core == p)

time: 111 us -> 110 us (level)
    pallas_call x1, Pallas kernels: 108 us -> 107 us  [shards(): pl.pallas_call(kernel, out_shape=jax.ShapeDtypeStruct((1, ROWS, COLS), bf...]
where the time goes in v4:
time: 110 us; the launch traced here: 109 us
  Pallas kernels  107 us (97%)
  local copies, waits for them, and re-layouts  1.58 us (1%)
    pallas_call x1, Pallas kernels, shards(): pl.pallas_call(kernel, out_shape=jax.ShapeDtypeStruct((1, ROWS, COLS), bf...  107 us

profile of v4, /device:TPU:1, one launch (start us, length us, event | category | flops | bytes accessed | tf_op | source)
XLA Modules:
  0.0 109.4 jit_solution(17580957536415591989)
XLA Ops:
  0.7 107.2 %shard_map.55 = bf16[1,112,640]{2,1,0:T(8,128)(2,1)} custom-call(s32[16]{0:T(128)} %owner_home.1, f32[1]{0:T(128)S(6)} %copy.7.damping, f32[1,112,3584]{2,1,0:T(8,128)} %factor.1, bf16[1,112,3584]{2,1,0:T(8,128)(2,1)} %inverse.1, bf16[1,112,640]{2,1,0:T(8,128)(2,1)} %acts.1), custom_call_target="tpu_custom_call" | custom-call | flops 1541406720 | bytes 3145728 | tf_op jit(solution)/shard_map/pallas_call | solution.py:437
  107.8 1.6 %copy.8 = bf16[1,112,640]{2,1,0:T(8,128)(2,1)} copy(bf16[1,112,640]{2,1,0:T(8,128)(2,1)} %shard_map.55) | data formatting | bytes 286720

commit v5 on v4

--- a/solution.py
+++ b/solution.py
@@ -18,7 +18,44 @@
 PARTS = (256, 384)
 FIRST = (0, 256)
 STREAMS = ((128, 128), (128, 128, 128))
-LONG_UP = (0, 3, 4, 6, 8)
+LONG_UP = (0, 1, 2, 7)
+A_STEPS = (
+    ((0, 1),),
+    ((0, 2),),
+    ((0, 3),),
+    ((0, 4),),
+    ((0, 5),),
+    ((0, 6),),
+    ((0, 7), (1, 1)),
+    ((0, 8), (1, 2)),
+    ((1, 3),),
+    ((1, 4),),
+    ((1, 5),),
+    ((1, 6),),
+    ((1, 7),),
+    ((1, 8),),
+    (),
+    (),
+)
+PRODUCTS = (
+    (),
+    ((0, 0, 0), (0, 0, 1), (0, 0, 2)),
+    ((0, 0, 3),),
+    ((0, 0, 4),),
+    ((0, 0, 5),),
+    (),
+    (),
+    (),
+    ((0, 0, 6), (0, 0, 7), (0, 0, 8), (0, 1, 0)),
+    ((2, 0, 0), (2, 0, 1), (2, 0, 2), (1, 0, 0), (1, 0, 1)),
+    ((2, 0, 3), (1, 0, 2), (1, 0, 3), (1, 0, 4), (1, 0, 5), (1, 0, 6), (1, 0, 7), (1, 0, 8), (1, 1, 0)),
+    ((2, 0, 4), (0, 1, 1), (1, 1, 1), (0, 1, 2), (1, 1, 2), (0, 1, 3), (1, 1, 3)),
+    ((2, 0, 5), (0, 1, 4), (1, 1, 4), (0, 1, 5), (1, 1, 5), (0, 1, 6), (1, 1, 6)),
+    ((2, 0, 6), (0, 1, 7), (1, 1, 7), (0, 1, 8), (1, 1, 8)),
+    ((2, 0, 7),),
+    (),
+)
+WHOLE = (11, 14)
 
 
 def wait_for(ref, sem):
@@ -27,7 +64,7 @@
 
 def kernel(
     owner_home, damping, factor, inverse, acts, out,
-    owner, f_in, p_in, f_out, p_out, f_work, p_work, a_own, a_ring,
+    owner, f_in, p_in, f_out, p_out, f_work, p_work, a_ring, a_w, p_a, p_a_sibling,
     w_ring, x_ring, total, sibling_part, fresh, gathered, picked,
     damp_out, damp_in, load_sem,
     swap_send, swap_recv, ring_send, ring_recv, pair_send, pair_recv,
@@ -110,21 +147,27 @@
         def _():
             wait_for(src, send)
 
-    w_home = [inverse.at[0, :, pl.ds(FIRST[p], PARTS[p])] for p in range(2)]
-    a_home = acts.at[0]
+    w_pieces, first = [], 0
+    for p in range(2):
+        for q, width in enumerate(STREAMS[p]):
+            w_pieces.append((p, q, first, width))
+            first += width
+    w_home = [inverse.at[0, :, pl.ds(first, width)] for p, q, first, width in w_pieces]
+    a_home = [acts.at[0, :, pl.ds(FIRST[p], PARTS[p])] for p in range(2)]
     own_rows = pl.ds(pl.multiple_of(side * ROWS, 16), ROWS)
 
-    for p in range(2):
-        keep(w_home[p], w_ring[p].at[z, pl.ds(0, ROWS)], swap_recv.at[8 * p], same)
-    keep(a_home, a_own.at[own_rows], swap_recv.at[1 + side], same)
+    for i, (p, q, _, _) in enumerate(w_pieces):
+        keep(w_home[i], w_ring[p][q].at[z, pl.ds(0, ROWS)], swap_recv.at[i], same)
+    for p in range(2):
+        keep(a_home[p], a_ring[p].at[z, pl.ds(0, ROWS)], swap_recv.at[5 + p], same)
 
     pad = jnp.zeros((KP - ROWS, COLS), jnp.bfloat16)
 
     def clear(i, carry):
         for p in range(2):
             a_ring[p][i, ROWS:KP, :] = pad[:, : PARTS[p]]
-            w_ring[p][i, ROWS:KP, :] = pad[:, : PARTS[p]]
             for q, width in enumerate(STREAMS[p]):
+                w_ring[p][q][i, ROWS:KP, :] = pad[:, :width]
                 x_ring[p][q][i, ROWS:KP, :] = pad[:, :width]
         return carry
 
@@ -156,19 +199,21 @@
 
     greet(0)
 
-    def swap_w(p):
+    def swap_w(i):
+        p, q = w_pieces[i][:2]
         deliver(
-            w_home[p], w_ring[p].at[z, pl.ds(0, ROWS)], swap_send.at[8 * p],
-            swap_recv.at[8 * p], at(side, core, z), same, True,
-        )
-
-    def swap_a(q, own):
+            w_home[i], w_ring[p][q].at[z, pl.ds(0, ROWS)], swap_send.at[i],
+            swap_recv.at[i], at(side, core, z), same, True,
+        )
+
+    def swap_a(p):
         deliver(
-            a_home, a_own.at[own_rows], swap_send.at[1 + q], swap_recv.at[1 + side],
-            at(side if q == 0 else 1 - side, core, z), own, True,
-        )
-
-    rings = [a_ring[0], a_ring[1], w_ring[0], w_ring[1]]
+            a_home[p], a_ring[p].at[z, pl.ds(0, ROWS)], swap_send.at[5 + p],
+            swap_recv.at[5 + p], at(side, core, z), same, True,
+        )
+
+    rings = [a_ring[0], a_ring[1]] + [w_ring[p][q] for p, q, _, _ in w_pieces]
+    w_streams = range(2, len(rings))
     streams_of = []
     for p in range(2):
         streams_of.append(range(len(rings), len(rings) + len(STREAMS[p])))
@@ -184,8 +229,7 @@
         return (z - hop + NZ) % NZ if way == 0 else (z + hop) % NZ
 
     def first_hop(stream):
-        p = stream % 2
-        home = w_home[p] if stream >= 2 else a_home.at[:, pl.ds(FIRST[p], PARTS[p])]
+        home = w_home[stream - 2] if stream >= 2 else a_home[stream]
         for way in range(2):
             pltpu.make_async_remote_copy(
                 src_ref=home, dst_ref=ring_ref(stream, z),
@@ -194,14 +238,12 @@
             ).start()
             pending.append(lambda r=home, m=ring_send.at[stream, way, 0]: wait_for(r, m))
 
-    first_hop(2)
+    for stream in w_streams:
+        first_hop(stream)
     first_hop(0)
-    first_hop(1)
-    first_hop(3)
-    swap_w(0)
-    swap_a(0, same)
-    swap_w(1)
-    swap_a(1, False)
+    for i in range(len(w_pieces)):
+        swap_w(i)
+    swap_a(0)
 
     damp_out[...] = jnp.full((8, 128), damping[0], jnp.float32)
 
@@ -209,8 +251,8 @@
     def _():
         damp_in[...] = damp_out[...]
         pltpu.make_async_remote_copy(
-            src_ref=damp_out, dst_ref=damp_in, send_sem=swap_send.at[7],
-            recv_sem=swap_recv.at[7], device_id=sibling, device_id_type=MESH,
+            src_ref=damp_out, dst_ref=damp_in, send_sem=swap_send.at[11],
+            recv_sem=swap_recv.at[11], device_id=sibling, device_id_type=MESH,
         ).start()
 
     def send_panel(src, dst, first):
@@ -238,44 +280,57 @@
                         lambda r=ref, m=ring_send.at[stream, way, hop]: wait_for(r, m)
                     )
 
-    def damp_block(place):
-        outer = sum(
-            lax.dot_general(
-                a_own[:, FIRST[p] : FIRST[p] + PARTS[p]], a_ring[p][place],
-                (((1,), (1,)), ((), ())), preferred_element_type=jnp.float32,
+    def rows_of(ring, places):
+        return jnp.concatenate([ring[place] for place in places], axis=0)
+
+    def lanes_of(panel, places):
+        return jnp.concatenate([panel[place] for place in places], axis=1)
+
+    def outer_product(p, places):
+        window = jnp.concatenate(
+            [rows_of(w_ring[i][q], places) for i, q, _, _ in w_pieces], axis=1
+        )
+        a_w[p][...] += lax.dot_general(
+            rows_of(a_ring[p], places), window, (((0,), (0,)), ((), ())),
+            preferred_element_type=jnp.float32,
+        )
+
+    def acts_product(p, places):
+        p_a[p][...] += jnp.dot(
+            lanes_of(p_work, places), rows_of(a_ring[p], places),
+            preferred_element_type=jnp.float32,
+        )
+
+    def panel_product(panel, ring, p, places):
+        first = 0
+        blocks = lanes_of(panel, places)
+        for q, width in enumerate(STREAMS[p]):
+            total[p][:, first : first + width] += jnp.dot(
+                blocks, rows_of(ring[p][q], places), preferred_element_type=jnp.float32
             )
-            for p in range(2)
-        )
-        damped = BETA * f_work[place].astype(jnp.float32) + ((1.0 - BETA) / TOK) * outer
-        f_work[place] = damped.astype(jnp.bfloat16)
-
-    def first_product(p):
-        def product(place):
-            total[p][...] += jnp.dot(
-                f_work[place], w_ring[p][place], preferred_element_type=jnp.float32
-            )
-        return product
-
-    def second_product(p):
-        def product(place):
-            first = 0
-            for q, width in enumerate(STREAMS[p]):
-                total[p][:, first : first + width] += jnp.dot(
-                    p_work[place], x_ring[p][q][place], preferred_element_type=jnp.float32
-                )
-                first += width
-        return product
-
-    def both(product, hop):
-        if hop == 0:
-            product(z)
-        elif hop == HOPS:
-            product((z + HOPS) % NZ)
+            first += width
+
+    def first_product(p, places):
+        panel_product(f_work, w_ring, p, places)
+
+    def second_product(p, places):
+        panel_product(p_work, x_ring, p, places)
+
+    def both(product, p, hop):
+        if hop == 0 or hop == HOPS:
+            product(p, [(z + hop) % NZ])
         else:
-            def one(s, carry):
-                product((z + NZ + (1 - 2 * s) * hop) % NZ)
-                return carry
-            lax.fori_loop(0, 2, one, 0)
+            product(p, [(z + NZ - hop) % NZ, (z + hop) % NZ])
+
+    def work(g):
+        for kind, p, hop in PRODUCTS[g - 1]:
+            if kind == 0:
+                both(outer_product, p, hop)
+            elif kind == 1:
+                both(acts_product, p, hop)
+            else:
+                for q in range(2):
+                    both(second_product, q, hop)
 
     mine = pl.ds(pl.multiple_of(core * ROWS, 16), ROWS)
     other = pl.ds(pl.multiple_of((1 - core) * ROWS, 16), ROWS)
@@ -289,58 +344,65 @@
 
     f_load.wait()
     relayout(f_in, f_out)
-    send_panel(f_out, f_work, 3)
+    send_panel(f_out, f_work, 7)
     p_load.wait()
     owner_load.wait()
     relayout(p_in, p_out)
     for p in range(2):
         total[p][...] = jnp.zeros_like(total[p])
 
-    done = [0, 0]
-
-    def catch_up(p, hop):
-        for _ in range(2):
-            if done[p] <= hop:
-                if p == 0:
-                    both(damp_block, done[p])
-                both(first_product(p), done[p])
-                done[p] += 1
+    for p in range(2):
+        p_a[p][...] = jnp.zeros_like(p_a[p])
+        a_w[p][...] = jnp.zeros_like(a_w[p])
 
     for hop in range(1, HOPS + 1):
-        for stream in (2, 0, 1):
+        for stream in w_streams:
             step(stream, hop)
-        if hop < HOPS:
-            step(3, hop)
+        if hop == HOPS:
+            for p in range(2):
+                both(first_product, p, hop)
+                pair_copy(p, 0).start()
+        else:
+            for p, h in A_STEPS[hop - 1]:
+                step(p, h)
         if hop in (2, 4, 6):
             greeted(hop // 2 - 1)
             if hop < 6:
                 greet(hop // 2)
+        if hop == 4:
+            swap_a(1)
+            first_hop(1)
         if hop == 2:
-            for p in range(2):
-                wait_for(w_ring[p].at[z, pl.ds(0, ROWS)], swap_recv.at[8 * p])
-            wait_for(a_own.at[mine], swap_recv.at[1 + core])
-            for p in range(2):
-                a_ring[p][z, 0:ROWS, :] = a_own[mine, FIRST[p] : FIRST[p] + PARTS[p]]
-        if hop == 4:
+            for i, (p, q, _, _) in enumerate(w_pieces):
+                wait_for(w_ring[p][q].at[z, pl.ds(0, ROWS)], swap_recv.at[i])
+            wait_for(a_ring[0].at[z, pl.ds(0, ROWS)], swap_recv.at[5])
+        if hop == 7:
+            wait_for(rings[1].at[z, pl.ds(0, ROWS)], swap_recv.at[6])
+        if hop == 3:
+            send_panel(p_out, p_work, 9)
+        if hop == 5:
             for b in range(2):
-                wait_for(f_work.at[:, pl.ds(b * ROWS, ROWS)], swap_recv.at[3 + b])
-            wait_for(a_own.at[other], swap_recv.at[2 - core])
-            send_panel(p_out, p_work, 5)
-        if hop >= 4:
-            catch_up(0, hop)
-            if hop == HOPS:
-                pair_copy(0, 0).start()
-                step(3, hop)
-            catch_up(1, hop)
+                wait_for(f_work.at[:, pl.ds(b * ROWS, ROWS)], swap_recv.at[7 + b])
+        if 5 <= hop < HOPS:
+            for h in range(3 * hop - 15, min(3 * hop - 12, HOPS)):
+                for p in range(2):
+                    both(first_product, p, h)
+        work(hop)
 
     @pl.when(jnp.logical_not(same))
     def _():
-        wait_for(damp_in, swap_recv.at[7])
+        wait_for(damp_in, swap_recv.at[11])
+
+    def own_window(p):
+        return jnp.concatenate(
+            [ring[z, 0:ROWS, :] for ring in w_ring[p]], axis=1
+        ).astype(jnp.float32)
 
     def apply(p):
         pair_copy(p, 0).wait()
-        window = w_ring[p][z, 0:ROWS, :].astype(jnp.float32)
-        applied = total[p][mine, :] + sibling_part[p][0] + damp_in[0:1, 0:1] * window
+        window = own_window(p)
+        applied = BETA * (total[p][mine, :] + sibling_part[p][0])
+        applied = applied + damp_in[0:1, 0:1] * window
         applied = applied.astype(jnp.bfloat16)
         first = 0
         for q, width in enumerate(STREAMS[p]):
@@ -349,31 +411,54 @@
             first += width
         total[p][...] = jnp.zeros_like(total[p])
 
-    pair_copy(1, 0).start()
     apply(0)
     apply(1)
-    for b in range(2):
-        wait_for(p_work.at[:, pl.ds(b * ROWS, ROWS)], swap_recv.at[5 + b])
-    for p in range(2):
-        both(second_product(p), 0)
+    for p, h in A_STEPS[HOPS - 1]:
+        step(p, h)
+
+    def acts_copy(p):
+        return pltpu.make_async_remote_copy(
+            src_ref=p_a[p], dst_ref=p_a_sibling[p], send_sem=pair_send.at[p, 2],
+            recv_sem=pair_recv.at[p, 2], device_id=sibling, device_id_type=MESH,
+        )
+
+    def join(p):
+        acts_copy(p).wait()
+        rows = ((1.0 - BETA) / TOK) * (p_a[p][...] + p_a_sibling[p][...])
+        share = jnp.dot(
+            rows.astype(jnp.bfloat16), a_w[p][...].astype(jnp.bfloat16),
+            preferred_element_type=jnp.float32,
+        )
+        for q in range(2):
+            total[q][...] += share[:, FIRST[q] : FIRST[q] + PARTS[q]]
+
     early, pending[:] = list(pending), []
     for hop in range(1, HOPS + 1):
+        if hop == HOPS:
+            join(0)
+            join(1)
         for p in range(2):
             for stream in streams_of[p]:
                 step(stream, hop)
             if hop == HOPS:
-                both(second_product(p), hop)
+                both(second_product, p, hop)
                 pair_copy(p, 1).start()
-        if hop < HOPS:
-            for p in range(2):
-                both(second_product(p), hop)
+        for p, h in A_STEPS[HOPS + hop - 1]:
+            step(p, h)
+        if hop == 2:
+            for b in range(2):
+                wait_for(p_work.at[:, pl.ds(b * ROWS, ROWS)], swap_recv.at[9 + b])
+        work(HOPS + hop)
+        for p in range(2):
+            if WHOLE[p] == HOPS + hop:
+                acts_copy(p).start()
         for left in early[(hop - 1) * len(early) // 6 : hop * len(early) // 6]:
             left()
 
     layer = chip * 2 + side
     for p in range(2):
         pair_copy(p, 1).wait()
-        window = w_ring[p][z, 0:ROWS, :].astype(jnp.float32)
+        window = own_window(p)
         fresh[p][...] = (
             2.0 * window - (total[p][mine, :] + sibling_part[p][1])
         ).astype(jnp.bfloat16)
@@ -412,7 +497,7 @@
 
     @pl.when(same)
     def _():
-        wait_for(damp_out, swap_send.at[7])
+        wait_for(damp_out, swap_send.at[11])
 
     for p in range(2):
         @pl.when(middle(p))
@@ -430,7 +515,7 @@
 def shards(owner, factor, inverse_old, acts_t, damping):
     bf16, f32 = jnp.bfloat16, jnp.float32
     dma, vmem = pltpu.SemaphoreType.DMA, pltpu.VMEM
-    n_streams = 4 + sum(len(widths) for widths in STREAMS)
+    n_streams = 2 + 2 * sum(len(widths) for widths in STREAMS)
     width = factor.shape[2]
     smem = pl.BlockSpec(memory_space=pltpu.SMEM)
     anywhere = pl.BlockSpec(memory_space=pltpu.HBM)
@@ -447,9 +532,11 @@
             vmem((2, NZ, ROWS, KP), bf16),
             vmem((NZ, 2 * ROWS, KP), bf16),
             vmem((NZ, 2 * ROWS, KP), bf16),
-            vmem((2 * ROWS, TOK), bf16),
             [vmem((NZ, KP, n), bf16) for n in PARTS],
-            [vmem((NZ, KP, n), bf16) for n in PARTS],
+            [vmem((n, COLS), f32) for n in PARTS],
+            [vmem((2 * ROWS, n), f32) for n in PARTS],
+            [vmem((2 * ROWS, n), f32) for n in PARTS],
+            [[vmem((NZ, KP, n), bf16) for n in widths] for widths in STREAMS],
             [[vmem((NZ, KP, n), bf16) for n in widths] for widths in STREAMS],
             [vmem((2 * ROWS, n), f32) for n in PARTS],
             [vmem((2, ROWS, n), f32) for n in PARTS],
@@ -459,12 +546,12 @@
             vmem((8, 128), f32),
             vmem((8, 128), f32),
             dma((3,)),
-            dma((9,)),
-            dma((9,)),
+            dma((12,)),
+            dma((12,)),
             dma((n_streams, 2, HOPS)),
             dma((n_streams, NZ)),
-            dma((2, 2)),
-            dma((2, 2)),
+            dma((2, 3)),
+            dma((2, 3)),
             dma((2, PIECES)),
             dma((2, NS)),
             dma((2, NS)),

time: 110 us -> 107 us (0.973)
  Pallas kernels: 107 us -> 105 us
    pallas_call x1, Pallas kernels: 107 us -> 105 us  [shards(): pl.pallas_call(kernel, out_shape=jax.ShapeDtypeStruct((1, ROWS, COLS), bf...]
where the time goes in v5:
time: 107 us
  Pallas kernels  105 us (98%)
  local copies, waits for them, and re-layouts  1.58 us (1%)
    pallas_call x1, Pallas kernels, shards(): pl.pallas_call(kernel, out_shape=jax.ShapeDtypeStruct((1, ROWS, COLS), bf...  105 us

profile of v5, /device:TPU:1, one launch (start us, length us, event | category | flops | bytes accessed | tf_op | source)
XLA Modules:
  0.0 106.9 jit_solution(6710339122426119190)
XLA Ops:
  0.7 104.7 %shard_map.55 = bf16[1,112,640]{2,1,0:T(8,128)(2,1)} custom-call(s32[16]{0:T(128)} %owner_home.1, f32[1]{0:T(128)S(6)} %copy.7.damping, f32[1,112,3584]{2,1,0:T(8,128)} %factor.1, bf16[1,112,3584]{2,1,0:T(8,128)(2,1)} %inverse.1, bf16[1,112,640]{2,1,0:T(8,128)(2,1)} %acts.1), custom_call_target="tpu_custom_call" | custom-call | flops 1541406720 | bytes 3145728 | tf_op jit(solution)/shard_map/pallas_call | solution.py:522
  105.3 1.6 %copy.8 = bf16[1,112,640]{2,1,0:T(8,128)(2,1)} copy(bf16[1,112,640]{2,1,0:T(8,128)(2,1)} %shard_map.55) | data formatting | bytes 286720

commit v6 on v5

--- a/solution.py
+++ b/solution.py
@@ -18,7 +18,7 @@
 PARTS = (256, 384)
 FIRST = (0, 256)
 STREAMS = ((128, 128), (128, 128, 128))
-LONG_UP = (0, 1, 2, 7)
+LONG_UP = (0, 1, 2, 4, 7, 9)
 A_STEPS = (
     ((0, 1),),
     ((0, 2),),

time: 107 us -> 107 us (level)
  no operation moved by 1% of the time
where the time goes in v6:
time: 107 us
  Pallas kernels  105 us (98%)
  local copies, waits for them, and re-layouts  1.58 us (1%)
    pallas_call x1, Pallas kernels, shards(): pl.pallas_call(kernel, out_shape=jax.ShapeDtypeStruct((1, ROWS, COLS), bf...  105 us

profile of v6, /device:TPU:1, one launch (start us, length us, event | category | flops | bytes accessed | tf_op | source)
XLA Modules:
  0.0 106.9 jit_solution(1315039981888568371)
XLA Ops:
  0.7 104.7 %shard_map.55 = bf16[1,112,640]{2,1,0:T(8,128)(2,1)} custom-call(s32[16]{0:T(128)} %owner_home.1, f32[1]{0:T(128)S(6)} %copy.7.damping, f32[1,112,3584]{2,1,0:T(8,128)} %factor.1, bf16[1,112,3584]{2,1,0:T(8,128)(2,1)} %inverse.1, bf16[1,112,640]{2,1,0:T(8,128)(2,1)} %acts.1), custom_call_target="tpu_custom_call" | custom-call | flops 1541406720 | bytes 3145728 | tf_op jit(solution)/shard_map/pallas_call | solution.py:522
  105.4 1.6 %copy.8 = bf16[1,112,640]{2,1,0:T(8,128)(2,1)} copy(bf16[1,112,640]{2,1,0:T(8,128)(2,1)} %shard_map.55) | data formatting | bytes 286720
